TPU v7x, 512 devices: a whole 4x8x8 slice. The times are simulated.
512 devices in a mesh: section: 16 (over y, core), tp: 32 (over z, x).
Axes of the slice: x: 4, y: 8, z: 8, core: 2. Of those that a mesh axis runs over, the one named last changes fastest.
Arguments:
- hidden: bfloat16 [16, 2, 256, 8192], P('section', None, None, 'tp'), may hold values from -400 to 400
- gain: float32 [16, 8192], P('section', 'tp'), may hold values from 0.5 to 1.5
- key_grad: bfloat16 [16, 2, 256, 1024], P('section', None, 'tp'), may hold values from -24 to 24
- master: float32 [16, 8192, 1024], P('section', 'tp'), may hold values from -0.0625 to 0.0625
- moment: float32 [16, 8192, 1024], P('section', 'tp'), may hold values from -0.00048828125 to 0.00048828125
- second: float32 [16, 8192, 1024], P('section', 'tp'), may hold values from 2.2351742e-11 to 2.23517418e-10
- overflow: int32 [16], P('section'), may hold values from 0 to 2
Outputs:
- grad_input: bfloat16 [16, 2, 256, 8192], P('section', None, None, 'tp')
- step: float32 [16, 8192, 1024], P('section', 'tp')
All inputs are finite; a program needn't handle non-finite values.
Results may differ from a plain program's by a relative error of at most 0.0049.
Values may be sent and summed in bfloat16 or wider, within the bound.
No kernel may reach another device: no remote copies, remote signals or barrier semaphores. Data moves between devices by JAX's collectives and lax.ppermute only.
A program may use at most 64 MiB of HBM per device.

v0:
```python
import jax
import jax.numpy as jnp
from jax import lax
from jax.experimental import pallas as pl
from jax.experimental.pallas import tpu as pltpu
from jax.sharding import Mesh, PartitionSpec as P

D = 8192
SEC, NZ, NX = 16, 8, 4
TP = NZ * NX
TOK = 512
F = 256
K = 1024
f32, bf16 = jnp.float32, jnp.bfloat16

beta_one = 0.9
beta_two = 0.999
decay = 0.1
clip_norm = 1.0
step_count = 10

VM = pl.BlockSpec(memory_space=pltpu.VMEM)
SM = pl.BlockSpec(memory_space=pltpu.SMEM)


def call(body, out_shape, n_in, flops=0, data=0, scratch=(), scalars=0):
    outs = (VM,) * len(out_shape) if isinstance(out_shape, tuple) else VM
    return pl.pallas_call(
        body,
        out_shape=out_shape,
        in_specs=[SM] * scalars + [VM] * n_in,
        out_specs=outs,
        scratch_shapes=list(scratch),
        compiler_params=pltpu.CompilerParams(vmem_limit_bytes=32 * 1024 * 1024),
        cost_estimate=pl.CostEstimate(flops=flops, bytes_accessed=data, transcendentals=0),
    )


def sds(shape, dtype=f32):
    return jax.ShapeDtypeStruct(shape, dtype)


def swap(blocks, axis):
    return lax.all_to_all(blocks, axis, split_axis=0, concat_axis=0, tiled=True)


def split_rows(row):
    rows = jnp.concatenate([row[:, i * 128 : (i + 1) * 128] for i in range(4)], axis=0)
    high = rows.astype(bf16).astype(f32)
    low = rows - high
    return jnp.concatenate([high, low, jnp.zeros((8, 128), f32)], axis=0).astype(bf16)


def join_rows(rows):
    rows = rows.astype(f32)
    return rows[0:4] + rows[4:8]


def as_row(rows):
    return jnp.concatenate([rows[i : i + 1] for i in range(4)], axis=1)


def features_first(x_ref):
    x = x_ref[...].astype(f32).reshape(2, TP, 8, F)
    return jnp.concatenate([x[0][:, None], x[1][:, None]], axis=1).reshape(TOK, F).T


def first_kernel(x_ref, key_ref, send_ref):
    xt = features_first(x_ref)
    sums = split_rows(jnp.sum(xt * xt, axis=0, keepdims=True))
    for peer in range(NZ):
        for c in range(8):
            send_ref[peer, c * 16 : (c + 1) * 16, :] = key_ref[:, c * 128 : (c + 1) * 128]
        send_ref[peer, 128:144, :] = sums


def middle_kernel(got_ref, send_ref):
    total = jnp.zeros((4, 128), f32)
    for z in range(NZ):
        total = total + join_rows(got_ref[z, 128:144, :])
    sums = split_rows(as_row(total))
    for peer in range(NX):
        for z in range(NZ):
            send_ref[peer, z * 128 : (z + 1) * 128, :] = got_ref[z, 0:128, :]
        send_ref[peer, 1024:1040, :] = sums


def main_kernel(
    factor_ref, x_ref, got_ref, gain_ref, master_ref, gw_ref, plain_ref, slope_ref, send_ref, rows_ref, gx_ref
):
    for x in range(NX):
        for z in range(NZ):
            slot = z * NX + x
            for c in range(8):
                rows_ref[slot * 16 : (slot + 1) * 16, c * 128 : (c + 1) * 128] = got_ref[
                    x, z * 128 + c * 16 : z * 128 + (c + 1) * 16, :
                ]
    total = jnp.zeros((4, 128), f32)
    for x in range(NX):
        total = total + join_rows(got_ref[x, 1024:1040, :])
    inv = lax.rsqrt(as_row(total) * (1.0 / D) + 1e-05)
    col = jnp.broadcast_to(gain_ref[...], (8, F)).T[:, 0:1]
    xt = features_first(x_ref)
    gx = xt * col
    gx_ref[...] = (gx * inv).astype(bf16)
    slope_ref[...] = xt * (inv * inv * inv * (1.0 / D))
    factor = factor_ref[0]
    square = jnp.zeros((1, 256), f32)
    for n in range(4):
        cols = slice(n * 256, (n + 1) * 256)
        part = factor * jnp.dot(gx_ref[...], rows_ref[:, cols], preferred_element_type=f32)
        gw_ref[:, cols] = part
        square = square + jnp.sum(part * part, axis=0, keepdims=True)
    own_sq = jnp.broadcast_to(jnp.sum(square, axis=1, keepdims=True), (4, 128))
    weight = master_ref[...].astype(bf16)
    parts = []
    for n in range(2):
        cols = slice(n * 256, (n + 1) * 256)
        gh = lax.dot_general(
            weight, rows_ref[cols, :], (((1,), (1,)), ((), ())), preferred_element_type=f32
        )
        plain_ref[:, cols] = inv[:, cols] * (col * gh)
        inner = jnp.sum(gx[:, cols] * gh, axis=0, keepdims=True)
        parts += [inner[:, 0:128], inner[:, 128:256]]
    packed = jnp.concatenate(parts + [own_sq], axis=0)
    for peer in range(TP):
        send_ref[peer] = packed


def branch_kernel(plain_ref, slope_ref, got_ref, send_ref):
    packed = got_ref[0]
    for peer in range(1, TP):
        packed = packed + got_ref[peer]
    sent = (plain_ref[...] - slope_ref[...] * as_row(packed[0:4])).astype(bf16)
    layer_sq = split_rows(jnp.concatenate([packed[4:5]] * 4, axis=1))
    for j in range(SEC):
        for q in range(4):
            send_ref[j, q * 16 : (q + 1) * 16, :] = sent[j * 16 : (j + 1) * 16, q * 128 : (q + 1) * 128]
        send_ref[j, 64:72, :] = layer_sq[0:8]


def suffix_kernel(got_ref, back_ref, clip_ref):
    running = jnp.zeros((64, 128), f32)
    norm = jnp.zeros((4, 128), f32)
    for s in range(SEC - 1, -1, -1):
        running = running + got_ref[s, 0:64, :].astype(f32)
        back_ref[s] = running.astype(bf16)
        norm = norm + join_rows(got_ref[s, 64:72, :])
    clip = jnp.minimum(1.0, clip_norm / (jnp.sqrt(norm) + 1e-06))
    clip_ref[...] = jnp.concatenate([clip, clip], axis=0)


def last_kernel(back_ref, out_ref):
    rows = []
    for j in range(SEC):
        rows.append(jnp.concatenate([back_ref[j, q * 16 : (q + 1) * 16, :] for q in range(4)], axis=1))
    out = jnp.concatenate(rows, axis=0).astype(f32).T.reshape(TP, 2, 8, F)
    for m in range(2):
        out_ref[m] = out[:, m].reshape(256, F).astype(bf16)


def on_device(hidden, gain, key_grad, master, moment, second, overflow):
    flag = overflow[0]
    factor = jnp.where(flag == 0, 1.0, jnp.where(flag == 1, 0.5, 0.0)).astype(f32)
    keep = jnp.where(flag == 2, 0.0, 1.0).astype(f32)

    send = call(first_kernel, sds((NZ, 144, 128), bf16), 2, 3 * F * TOK, F * TOK * 2)(
        hidden[0], key_grad.reshape(16, K)
    )
    got = swap(send, "z")
    send = call(middle_kernel, sds((NX, 1040, 128), bf16), 1, 0, 1024 * 1024)(got)
    got = swap(send, "x")
    gw, plain, slope, send = call(
        main_kernel,
        (sds((F, K)), sds((F, TOK)), sds((F, TOK)), sds((TP, 8, 128))),
        4,
        4 * F * TOK * K,
        4 * 1024 * 1024,
        [pltpu.VMEM((TOK, K), bf16), pltpu.VMEM((F, TOK), bf16)],
        1,
    )(factor[None], hidden[0], got, gain, master[0])
    got = swap(send, ("z", "x"))
    send = call(branch_kernel, sds((SEC, 72, 128), bf16), 3, 3 * F * TOK, 1024 * 1024)(plain, slope, got)
    got = swap(send, ("y", "core"))
    back, clip = call(
        suffix_kernel, (sds((SEC, 64, 128), bf16), sds((8, 128))), 1, 4 * F * TOK, 1024 * 1024
    )(got)
    back = swap(back, ("y", "core"))
    clipped = clip[0, 0] * gw
    moment_new = beta_one * moment[0] + (1.0 - beta_one) * clipped
    second_new = beta_two * second[0] + (1.0 - beta_two) * clipped * clipped
    bias_one = 1.0 - beta_one**step_count
    bias_two = 1.0 - beta_two**step_count
    update = moment_new / bias_one / (jnp.sqrt(second_new / bias_two) + 1e-08) + decay * master[0]
    grad_input = call(last_kernel, sds((2, 256, F), bf16), 1, F * TOK, 1024 * 1024)(back)
    return (grad_input[None], (keep * update)[None])


def solution(mesh):
    fine = Mesh(mesh.devices.reshape(8, 2, NZ, NX), ("y", "core", "z", "x"))
    sec, tp = ("y", "core"), ("z", "x")
    return jax.shard_map(
        on_device,
        mesh=fine,
        in_specs=(
            P(sec, None, None, tp),
            P(sec, tp),
            P(sec, None, tp, None),
            P(sec, tp, None),
            P(sec, tp, None),
            P(sec, tp, None),
            P(sec),
        ),
        out_specs=(P(sec, None, None, tp), P(sec, tp, None)),
        check_vma=False,
    )
```

profile of v0, /device:TPU:1, one launch (start us, length us, event | category | flops | bytes accessed | tf_op | source)
XLA Modules:
  0.0 97.0 jit_solution(3142912856081876028)
XLA Ops:
  0.6 0.0 copy-start.1
  0.6 0.9 copy-done.1
  1.6 0.0 copy-start.3
  1.6 0.8 copy-done.3
  2.3 0.2 shard_map.86
  2.5 21.5 %all_to_all.25.got_ref = bf16[8,144,128]{2,1,0:T(8,128)(2,1)S(1)} all-to-all(bf16[8,144,128]{2,1,0:T(8,128)(2,1)S(1)} %shard_map.86), channel_id=1, replica_groups=mesh['y'=8,'core'=2,'z'=8,'x'=4] {'z'}, dimensions={0} | all-to-all | bytes 589824 | tf_op jit(solution)/shard_map/all_to_all | solution.py:44
  24.0 1.1 %shard_map.87 = bf16[4,1040,128]{2,1,0:T(8,128)(2,1)} custom-call(bf16[8,144,128]{2,1,0:T(8,128)(2,1)S(1)} %all_to_all.25.got_ref), custom_call_target="tpu_custom_call" | custom-call | bytes 1048576 | tf_op jit(solution)/shard_map/pallas_call | solution.py:171
  25.1 4.1 %all-to-all-start.1 = ((bf16[4,1040,128]{2,1,0:T(8,128)(2,1)}), bf16[4,1040,128]{2,1,0:T(8,128)(2,1)S(1)}, u32[]{:S(2)}, u32[]{:S(2)}) async-start(bf16[4,1040,128]{2,1,0:T(8,128)(2,1)} %shard_map.87), calls=%async_computation.1 | async-start | bytes 2129920 | tf_op jit(solution)/shard_map/all_to_all | solution.py:44
  29.9 11.4 %all-to-all-done.1.got_ref = bf16[4,1040,128]{2,1,0:T(8,128)(2,1)S(1)} async-done(((bf16[4,1040,128]{2,1,0:T(8,128)(2,1)}), bf16[4,1040,128]{2,1,0:T(8,128)(2,1)S(1)}, u32[]{:S(2)}, u32[]{:S(2)}) %all-to-all-start.1) | async-done | bytes 1064992 | tf_op jit(solution)/shard_map/all_to_all | solution.py:44
  41.3 0.0 copy-done
  41.3 0.0 copy-done.2
  41.3 0.0 copy-done.4
  41.3 1.0 %shard_map.88 = (f32[256,1024]{1,0:T(8,128)S(1)}, f32[256,512]{1,0:T(8,128)S(1)}, f32[256,512]{1,0:T(8,128)S(1)}, f32[32,8,128]{2,1,0:T(8,128)S(1)}) custom-call(f32[1]{0:T(128)S(6)} %select_n.17.factor_ref, bf16[2,256,256]{2,1,0:T(8,128)(2,1)S(1)} %bitcast.23, bf16[4,1040,128]{2,1,0:T(8,128)(2,1)S(1)} %all-to-all-done.1.got_ref, f32[1,256]{1,0:T(1,128)S(1)} %copy-done.4, ...), custom_call_target="tpu_custom_call" | custom-call | flops 536870912 | bytes 4194304 | tf_op jit(solution)/shard_map/pallas_call | solution.py:173
  42.3 15.3 %all_to_all.26.got_ref = f32[32,8,128]{2,1,0:T(8,128)S(1)} all-to-all(f32[32,8,128]{2,1,0:T(8,128)S(1)} %get-tuple-element.10), channel_id=1, replica_groups=mesh['y'=8,'core'=2,'z'=8,'x'=4] {'z','x'}, dimensions={0} | all-to-all | bytes 262144 | tf_op jit(solution)/shard_map/all_to_all | solution.py:44
  57.6 0.1 shard_map.89
  57.7 0.0 copy-start.5
  57.7 23.1 %all_to_all.27.got_ref = bf16[16,72,128]{2,1,0:T(8,128)(2,1)S(1)} all-to-all(bf16[16,72,128]{2,1,0:T(8,128)(2,1)S(1)} %shard_map.89), channel_id=1, replica_groups=mesh['y'=8,'core'=2,'z'=8,'x'=4] {'y','core'}, dimensions={0} | all-to-all | bytes 589824 | tf_op jit(solution)/shard_map/all_to_all | solution.py:44
  80.8 0.7 shard_map.90
  81.5 3.4 %all-to-all-start.4 = ((bf16[16,64,128]{2,1,0:T(8,128)(2,1)}), bf16[16,64,128]{2,1,0:T(8,128)(2,1)S(1)}, u32[]{:S(2)}, u32[]{:S(2)}) async-start(bf16[16,64,128]{2,1,0:T(8,128)(2,1)} %get-tuple-element.11), calls=%async_computation.4 | async-start | bytes 524288 | tf_op jit(solution)/shard_map/all_to_all | solution.py:44
  85.0 0.6 slice.3
  85.6 0.0 copy-done.5
  85.6 3.6 %multiply_bitcast_fusion = f32[1,256,1024]{2,1,0:T(8,128)} fusion(f32[1,256,1024]{2,1,0:T(8,128)S(1)} %copy-done.5, f32[256,1024]{1,0:T(8,128)S(1)} %get-tuple-element.13, f32[1,256,1024]{2,1,0:T(8,128)} %param.11, f32[]{:T(128)} %bitcast.6, f32[]{:T(128)} %bitcast.4, f32[1,256,1024]{2,1,0:T(8,128)S(1)} %copy-done), kind=kLoop, calls=%fused_computation.9 | loop fusion | flops 3932160 | bytes 5242888 | tf_op jit(solution)/shard_map/broadcast_in_dim | solution.py:196
  89.2 7.0 %all-to-all-done.4.back_ref = bf16[16,64,128]{2,1,0:T(8,128)(2,1)S(1)} async-done(((bf16[16,64,128]{2,1,0:T(8,128)(2,1)}), bf16[16,64,128]{2,1,0:T(8,128)(2,1)S(1)}, u32[]{:S(2)}, u32[]{:S(2)}) %all-to-all-start.4) | async-done | bytes 262176 | tf_op jit(solution)/shard_map/all_to_all | solution.py:44
  96.1 0.8 shard_map.91
  (3 shorter events, 0.0 us)
Async XLA Ops:
  0.6 1.0 copy-start.1
  1.6 0.8 copy-start.3
  25.1 16.2 %copy-start = (f32[1,256,1024]{2,1,0:T(8,128)S(1)}, f32[1,256,1024]{2,1,0:T(8,128)}, u32[]{:S(2)}) copy-start(f32[1,256,1024]{2,1,0:T(8,128)} %param.10) | copy-start | bytes 3145732
  25.1 16.2 %copy-start.2 = (bf16[1,2,256,256]{3,2,1,0:T(8,128)(2,1)S(1)}, bf16[1,2,256,256]{3,2,1,0:T(8,128)(2,1)}, u32[]{:S(2)}) copy-start(bf16[1,2,256,256]{3,2,1,0:T(8,128)(2,1)} %param.7) | copy-start | bytes 786436
  25.1 16.2 %copy-start.4 = (f32[1,256]{1,0:T(1,128)S(1)}, f32[1,256]{1,0:T(1,128)}, u32[]{:S(2)}) copy-start(f32[1,256]{1,0:T(1,128)} %gain_ref.1) | copy-start | bytes 3076
  25.1 16.2 %all-to-all-start.1 = ((bf16[4,1040,128]{2,1,0:T(8,128)(2,1)}), bf16[4,1040,128]{2,1,0:T(8,128)(2,1)S(1)}, u32[]{:S(2)}, u32[]{:S(2)}) async-start(bf16[4,1040,128]{2,1,0:T(8,128)(2,1)} %shard_map.87), calls=%async_computation.1 | async-start | bytes 2129920 | tf_op jit(solution)/shard_map/all_to_all | solution.py:44
  57.7 27.9 %copy-start.5 = (f32[1,256,1024]{2,1,0:T(8,128)S(1)}, f32[1,256,1024]{2,1,0:T(8,128)}, u32[]{:S(2)}) copy-start(f32[1,256,1024]{2,1,0:T(8,128)} %param.12) | copy-start | bytes 3145732
  81.5 14.6 %all-to-all-start.4 = ((bf16[16,64,128]{2,1,0:T(8,128)(2,1)}), bf16[16,64,128]{2,1,0:T(8,128)(2,1)S(1)}, u32[]{:S(2)}, u32[]{:S(2)}) async-start(bf16[16,64,128]{2,1,0:T(8,128)(2,1)} %get-tuple-element.11), calls=%async_computation.4 | async-start | bytes 524288 | tf_op jit(solution)/shard_map/all_to_all | solution.py:44
where the time goes:
time: 97.5 us; the launch traced here: 97 us
  blocking collectives  59.9 us (61%)
  waiting for transfers between devices  18.3 us (19%)
  starting transfers between devices  7.57 us (8%)
  Pallas kernels  3.94 us (4%)
  other arithmetic  3.61 us (4%)
  local copies, waits for them, and re-layouts  2.3 us (2%)
  between operations  1.35 us (1%)
    all_to_all x3, blocking collectives, swap(): return lax.all_to_all(blocks, axis, split_axis=0, concat_axis=0, tiled=True)  59.9 us
    all_to_all x2, waiting for transfers between devices, swap(): return lax.all_to_all(blocks, axis, split_axis=0, concat_axis=0, tiled=True)  18.3 us
    all_to_all x2, starting transfers between devices, swap(): return lax.all_to_all(blocks, axis, split_axis=0, concat_axis=0, tiled=True)  7.57 us
    broadcast_in_dim x1, other arithmetic, on_device(): return (grad_input[None], (keep * update)[None])  3.61 us
  transfers between devices with their start and end apart: 2, of which 2 were waited for; matrix products, arithmetic and copies ran while one was open for 4% of the time, Pallas kernels for 0%

commit v1 on v0

--- a/solution.py
+++ b/solution.py
@@ -111,7 +111,7 @@
         part = factor * jnp.dot(gx_ref[...], rows_ref[:, cols], preferred_element_type=f32)
         gw_ref[:, cols] = part
         square = square + jnp.sum(part * part, axis=0, keepdims=True)
-    own_sq = jnp.broadcast_to(jnp.sum(square, axis=1, keepdims=True), (4, 128))
+    own_sq = jnp.broadcast_to(jnp.sum(square, axis=1, keepdims=True), (1, 128))
     weight = master_ref[...].astype(bf16)
     parts = []
     for n in range(2):
@@ -120,9 +120,8 @@
             weight, rows_ref[cols, :], (((1,), (1,)), ((), ())), preferred_element_type=f32
         )
         plain_ref[:, cols] = inv[:, cols] * (col * gh)
-        inner = jnp.sum(gx[:, cols] * gh, axis=0, keepdims=True)
-        parts += [inner[:, 0:128], inner[:, 128:256]]
-    packed = jnp.concatenate(parts + [own_sq], axis=0)
+        parts.append(jnp.sum(gx[:, cols] * gh, axis=0, keepdims=True))
+    packed = jnp.concatenate(parts + [own_sq], axis=1)
     for peer in range(TP):
         send_ref[peer] = packed
 
@@ -131,8 +130,8 @@
     packed = got_ref[0]
     for peer in range(1, TP):
         packed = packed + got_ref[peer]
-    sent = (plain_ref[...] - slope_ref[...] * as_row(packed[0:4])).astype(bf16)
-    layer_sq = split_rows(jnp.concatenate([packed[4:5]] * 4, axis=1))
+    sent = (plain_ref[...] - slope_ref[...] * packed[:, 0:TOK]).astype(bf16)
+    layer_sq = split_rows(jnp.concatenate([packed[:, TOK:]] * 4, axis=1))
     for j in range(SEC):
         for q in range(4):
             send_ref[j, q * 16 : (q + 1) * 16, :] = sent[j * 16 : (j + 1) * 16, q * 128 : (q + 1) * 128]
@@ -142,7 +141,8 @@
 def suffix_kernel(got_ref, back_ref, clip_ref):
     running = jnp.zeros((64, 128), f32)
     norm = jnp.zeros((4, 128), f32)
-    for s in range(SEC - 1, -1, -1):
+    for layer in range(SEC - 1, -1, -1):
+        s = layer % 2 * 8 + layer // 2
         running = running + got_ref[s, 0:64, :].astype(f32)
         back_ref[s] = running.astype(bf16)
         norm = norm + join_rows(got_ref[s, 64:72, :])
@@ -172,7 +172,7 @@
     got = swap(send, "x")
     gw, plain, slope, send = call(
         main_kernel,
-        (sds((F, K)), sds((F, TOK)), sds((F, TOK)), sds((TP, 8, 128))),
+        (sds((F, K)), sds((F, TOK)), sds((F, TOK)), sds((TP, 1, TOK + 128))),
         4,
         4 * F * TOK * K,
         4 * 1024 * 1024,
@@ -181,11 +181,11 @@
     )(factor[None], hidden[0], got, gain, master[0])
     got = swap(send, ("z", "x"))
     send = call(branch_kernel, sds((SEC, 72, 128), bf16), 3, 3 * F * TOK, 1024 * 1024)(plain, slope, got)
-    got = swap(send, ("y", "core"))
+    got = swap(send, ("core", "y"))
     back, clip = call(
         suffix_kernel, (sds((SEC, 64, 128), bf16), sds((8, 128))), 1, 4 * F * TOK, 1024 * 1024
     )(got)
-    back = swap(back, ("y", "core"))
+    back = swap(back, ("core", "y"))
     clipped = clip[0, 0] * gw
     moment_new = beta_one * moment[0] + (1.0 - beta_one) * clipped
     second_new = beta_two * second[0] + (1.0 - beta_two) * clipped * clipped

time: 97.5 us -> 95.3 us (0.977)
  blocking collectives: 59.9 us -> 57.1 us
  starting transfers between devices: 7.57 us -> 9.46 us
  waiting for transfers between devices: 18.3 us -> 16.6 us
    all_to_all x3, blocking collectives: 59.9 us -> 57.1 us  [swap(): return lax.all_to_all(blocks, axis, split_axis=0, concat_axis=0, tiled=True)]
    all_to_all x2, starting transfers between devices: 7.57 us -> 9.46 us  [swap(): return lax.all_to_all(blocks, axis, split_axis=0, concat_axis=0, tiled=True)]
    all_to_all x2, waiting for transfers between devices: 18.3 us -> 16.6 us  [swap(): return lax.all_to_all(blocks, axis, split_axis=0, concat_axis=0, tiled=True)]
where the time goes in v1:
time: 95.3 us; the launch traced here: 94.3 us
  blocking collectives  57.1 us (60%)
  waiting for transfers between devices  16.6 us (17%)
  starting transfers between devices  9.46 us (10%)
  Pallas kernels  3.94 us (4%)
  other arithmetic  3.61 us (4%)
  local copies, waits for them, and re-layouts  2.29 us (2%)
  between operations  1.33 us (1%)
    all_to_all x3, blocking collectives, swap(): return lax.all_to_all(blocks, axis, split_axis=0, concat_axis=0, tiled=True)  57.1 us
    all_to_all x2, waiting for transfers between devices, swap(): return lax.all_to_all(blocks, axis, split_axis=0, concat_axis=0, tiled=True)  16.6 us
    all_to_all x2, starting transfers between devices, swap(): return lax.all_to_all(blocks, axis, split_axis=0, concat_axis=0, tiled=True)  9.46 us
    broadcast_in_dim x1, other arithmetic, on_device(): return (grad_input[None], (keep * update)[None])  3.61 us
  transfers between devices with their start and end apart: 2, of which 2 were waited for; matrix products, arithmetic and copies ran while one was open for 4% of the time, Pallas kernels for 0%

profile of v1, /device:TPU:1, one launch (start us, length us, event | category | flops | bytes accessed | tf_op | source)
XLA Modules:
  0.0 94.3 jit_solution(3329798689963948200)
XLA Ops:
  0.6 0.0 copy-start.1
  0.6 0.9 copy-done.1
  1.6 0.0 copy-start.3
  1.6 0.8 copy-done.3
  2.3 0.2 shard_map.86
  2.5 21.5 %all_to_all.25.got_ref = bf16[8,144,128]{2,1,0:T(8,128)(2,1)S(1)} all-to-all(bf16[8,144,128]{2,1,0:T(8,128)(2,1)S(1)} %shard_map.86), channel_id=1, replica_groups=mesh['y'=8,'core'=2,'z'=8,'x'=4] {'z'}, dimensions={0} | all-to-all | bytes 589824 | tf_op jit(solution)/shard_map/all_to_all | solution.py:44
  24.0 1.1 %shard_map.87 = bf16[4,1040,128]{2,1,0:T(8,128)(2,1)} custom-call(bf16[8,144,128]{2,1,0:T(8,128)(2,1)S(1)} %all_to_all.25.got_ref), custom_call_target="tpu_custom_call" | custom-call | bytes 1048576 | tf_op jit(solution)/shard_map/pallas_call | solution.py:171
  25.1 4.1 %all-to-all-start.1 = ((bf16[4,1040,128]{2,1,0:T(8,128)(2,1)}), bf16[4,1040,128]{2,1,0:T(8,128)(2,1)S(1)}, u32[]{:S(2)}, u32[]{:S(2)}) async-start(bf16[4,1040,128]{2,1,0:T(8,128)(2,1)} %shard_map.87), calls=%async_computation.1 | async-start | bytes 2129920 | tf_op jit(solution)/shard_map/all_to_all | solution.py:44
  29.9 11.4 %all-to-all-done.1.got_ref = bf16[4,1040,128]{2,1,0:T(8,128)(2,1)S(1)} async-done(((bf16[4,1040,128]{2,1,0:T(8,128)(2,1)}), bf16[4,1040,128]{2,1,0:T(8,128)(2,1)S(1)}, u32[]{:S(2)}, u32[]{:S(2)}) %all-to-all-start.1) | async-done | bytes 1064992 | tf_op jit(solution)/shard_map/all_to_all | solution.py:44
  41.3 0.0 copy-done
  41.3 0.0 copy-done.2
  41.3 0.0 copy-done.4
  41.3 1.0 %shard_map.88 = (f32[256,1024]{1,0:T(8,128)S(1)}, f32[256,512]{1,0:T(8,128)S(1)}, f32[256,512]{1,0:T(8,128)S(1)}, f32[32,1,640]{2,1,0:T(1,128)S(1)}) custom-call(f32[1]{0:T(128)S(6)} %select_n.17.factor_ref, bf16[2,256,256]{2,1,0:T(8,128)(2,1)S(1)} %bitcast.23, bf16[4,1040,128]{2,1,0:T(8,128)(2,1)S(1)} %all-to-all-done.1.got_ref, f32[1,256]{1,0:T(1,128)S(1)} %copy-done.4, ...), custom_call_target="tpu_custom_call" | custom-call | flops 536870912 | bytes 4194304 | tf_op jit(solution)/shard_map/pallas_call | solution.py:173
  42.3 14.9 %all_to_all.26.got_ref = f32[32,1,640]{2,1,0:T(1,128)S(1)} all-to-all(f32[32,1,640]{2,1,0:T(1,128)S(1)} %get-tuple-element.10), channel_id=1, replica_groups=mesh['y'=8,'core'=2,'z'=8,'x'=4] {'z','x'}, dimensions={0} | all-to-all | bytes 163840 | tf_op jit(solution)/shard_map/all_to_all | solution.py:44
  57.2 0.1 shard_map.89
  57.3 0.0 copy-start.5
  57.3 20.7 %all_to_all.27.got_ref = bf16[16,72,128]{2,1,0:T(8,128)(2,1)S(1)} all-to-all(bf16[16,72,128]{2,1,0:T(8,128)(2,1)S(1)} %shard_map.89), channel_id=1, replica_groups=mesh['y'=8,'core'=2,'z'=8,'x'=4] {'core','y'}, dimensions={0} | all-to-all | bytes 589824 | tf_op jit(solution)/shard_map/all_to_all | solution.py:44
  78.0 0.7 shard_map.90
  78.8 5.3 %all-to-all-start.4 = ((bf16[16,64,128]{2,1,0:T(8,128)(2,1)}), bf16[16,64,128]{2,1,0:T(8,128)(2,1)S(1)}, u32[]{:S(2)}, u32[]{:S(2)}) async-start(bf16[16,64,128]{2,1,0:T(8,128)(2,1)} %get-tuple-element.11), calls=%async_computation.4 | async-start | bytes 524288 | tf_op jit(solution)/shard_map/all_to_all | solution.py:44
  84.1 0.6 slice.3
  84.7 0.0 copy-done.5
  84.7 3.6 %multiply_bitcast_fusion = f32[1,256,1024]{2,1,0:T(8,128)} fusion(f32[1,256,1024]{2,1,0:T(8,128)S(1)} %copy-done.5, f32[256,1024]{1,0:T(8,128)S(1)} %get-tuple-element.13, f32[1,256,1024]{2,1,0:T(8,128)} %param.11, f32[]{:T(128)} %bitcast.6, f32[]{:T(128)} %bitcast.4, f32[1,256,1024]{2,1,0:T(8,128)S(1)} %copy-done), kind=kLoop, calls=%fused_computation.9 | loop fusion | flops 3932160 | bytes 5242888 | tf_op jit(solution)/shard_map/broadcast_in_dim | solution.py:196
  88.3 5.2 %all-to-all-done.4.back_ref = bf16[16,64,128]{2,1,0:T(8,128)(2,1)S(1)} async-done(((bf16[16,64,128]{2,1,0:T(8,128)(2,1)}), bf16[16,64,128]{2,1,0:T(8,128)(2,1)S(1)}, u32[]{:S(2)}, u32[]{:S(2)}) %all-to-all-start.4) | async-done | bytes 262176 | tf_op jit(solution)/shard_map/all_to_all | solution.py:44
  93.5 0.8 shard_map.91
  (3 shorter events, 0.0 us)
Async XLA Ops:
  0.6 1.0 %copy-start.1 = (bf16[1,2,256,256]{3,2,1,0:T(8,128)(2,1)S(1)}, bf16[1,2,256,256]{3,2,1,0:T(8,128)(2,1)}, u32[]{:S(2)}) copy-start(bf16[1,2,256,256]{3,2,1,0:T(8,128)(2,1)} %param.7) | copy-start | bytes 786436
  1.6 0.8 copy-start.3
  25.1 16.2 %copy-start = (f32[1,256,1024]{2,1,0:T(8,128)S(1)}, f32[1,256,1024]{2,1,0:T(8,128)}, u32[]{:S(2)}) copy-start(f32[1,256,1024]{2,1,0:T(8,128)} %param.10) | copy-start | bytes 3145732
  25.1 16.2 %copy-start.2 = (bf16[1,2,256,256]{3,2,1,0:T(8,128)(2,1)S(1)}, bf16[1,2,256,256]{3,2,1,0:T(8,128)(2,1)}, u32[]{:S(2)}) copy-start(bf16[1,2,256,256]{3,2,1,0:T(8,128)(2,1)} %param.7) | copy-start | bytes 786436
  25.1 16.2 %copy-start.4 = (f32[1,256]{1,0:T(1,128)S(1)}, f32[1,256]{1,0:T(1,128)}, u32[]{:S(2)}) copy-start(f32[1,256]{1,0:T(1,128)} %gain_ref.1) | copy-start | bytes 3076
  25.1 16.2 %all-to-all-start.1 = ((bf16[4,1040,128]{2,1,0:T(8,128)(2,1)}), bf16[4,1040,128]{2,1,0:T(8,128)(2,1)S(1)}, u32[]{:S(2)}, u32[]{:S(2)}) async-start(bf16[4,1040,128]{2,1,0:T(8,128)(2,1)} %shard_map.87), calls=%async_computation.1 | async-start | bytes 2129920 | tf_op jit(solution)/shard_map/all_to_all | solution.py:44
  57.3 27.3 %copy-start.5 = (f32[1,256,1024]{2,1,0:T(8,128)S(1)}, f32[1,256,1024]{2,1,0:T(8,128)}, u32[]{:S(2)}) copy-start(f32[1,256,1024]{2,1,0:T(8,128)} %param.12) | copy-start | bytes 3145732
  78.8 14.7 %all-to-all-start.4 = ((bf16[16,64,128]{2,1,0:T(8,128)(2,1)}), bf16[16,64,128]{2,1,0:T(8,128)(2,1)S(1)}, u32[]{:S(2)}, u32[]{:S(2)}) async-start(bf16[16,64,128]{2,1,0:T(8,128)(2,1)} %get-tuple-element.11), calls=%async_computation.4 | async-start | bytes 524288 | tf_op jit(solution)/shard_map/all_to_all | solution.py:44
